TPU v7x, 256 devices: a whole 4x4x8 slice. The times are simulated.
256 devices in a mesh: ctx: 32 (over y, z), head: 8 (over x, core).
Axes of the slice: x: 4, y: 4, z: 8, core: 2. Of those that a mesh axis runs over, the one named last changes fastest.
Arguments:
- query: bfloat16 [16384, 64, 128], P('ctx', 'head'), may hold values from -6 to 6
- key: bfloat16 [16384, 64, 128], P('ctx', 'head'), may hold values from -6 to 6
- value: bfloat16 [16384, 64, 128], P('ctx', 'head'), may hold values from -40 to 40
- gain: float32 [64, 128], P('head'), may hold values from 0.1 to 1.9
- cotangent: bfloat16 [16384, 64, 128], P('ctx', 'head'), may hold values from -6 to 6
- query2: bfloat16 [16384, 64, 128], P('ctx', 'head'), may hold values from -5 to 5
- key2: bfloat16 [16384, 8, 128], P('ctx', 'head'), may hold values from -5 to 5
- softmax_values: bfloat16 [16384, 8, 128], P('ctx', 'head'), may hold values from -6 to 6
Outputs:
- normed: bfloat16 [16384, 64, 128], P('ctx', 'head')
- grad_query: bfloat16 [16384, 64, 128], P('ctx', 'head')
- grad_key: bfloat16 [16384, 64, 128], P('ctx', 'head')
- grad_value: bfloat16 [16384, 64, 128], P('ctx', 'head')
- attended: bfloat16 [16384, 64, 128], P('ctx', 'head')
All inputs are finite; a program needn't handle non-finite values.
Results may differ from a plain program's by a relative error of at most 0.02.
Values may be sent and summed in bfloat16 or wider, within the bound.
No kernel may reach another device: no remote copies, remote signals or barrier semaphores. Data moves between devices by JAX's collectives and lax.ppermute only.
A program may use at most 128 MiB of HBM per device.

v0:
```python
import jax
import jax.numpy as jnp
from jax import lax
from jax.sharding import PartitionSpec as P

ATTN_HEADS = 64
HEAD_WIDTH = 128
WINDOW_BLOCKS = 4


epsilon = 1e-06
high = lax.Precision.HIGHEST


def entering(value, axis, join, neutral, backward):
    count, mine = (lax.axis_size(axis), lax.axis_index(axis))
    pieces = lax.all_gather(value, axis)
    if backward:
        pieces = pieces[::-1]
        mine = count - 1 - mine
    so_far = jnp.full_like(value, 0) + jnp.asarray(neutral, value.dtype)

    def hop(position, so_far):
        longer = join(so_far, pieces[position])
        return jnp.where(position < mine, longer, so_far)

    return lax.fori_loop(0, count - 1, hop, so_far)


def from_behind(shard, axis, by):
    peers = lax.axis_size(axis)
    pairs = [(i, i + by) for i in range(peers) if 0 <= i + by < peers]
    return lax.ppermute(shard, axis, pairs)


def lower_mask(count):
    row_ids = lax.broadcasted_iota(jnp.int32, (count, count), 0)
    col_ids = lax.broadcasted_iota(jnp.int32, (count, count), 1)
    return col_ids <= row_ids


def add_states(earlier, later):
    return earlier + later


def local(query, key, value, gain, cotangent, query2, key2, softmax_values):
    block_rows = query.shape[0]
    head_count = query.shape[1]
    head_width = query.shape[2]
    position = lax.axis_index("ctx")
    causal = lower_mask(block_rows)[None]
    scores = jnp.einsum("thd,shd->hts", query, key, preferred_element_type=jnp.float32)
    weights = jnp.where(causal, scores, 0.0).astype(jnp.bfloat16)
    intra_part = jnp.einsum("hts,shd->thd", weights, value, preferred_element_type=jnp.float32)
    block_state = jnp.einsum("shi,shj->hij", key, value, preferred_element_type=jnp.float32)
    zero_state = jnp.zeros_like(block_state)
    prefix = entering(block_state, "ctx", add_states, zero_state, False)
    query_f = query.astype(jnp.float32)
    attention = intra_part + jnp.einsum("thi,hij->thj", query_f, prefix, precision=high)
    count = ATTN_HEADS * HEAD_WIDTH
    gain_b = gain[None]
    grad_in = gain_b * cotangent.astype(jnp.float32)
    local_squares = jnp.sum(attention * attention, axis=(1, 2))
    total_sq = lax.psum(local_squares, "head")
    inverse_rms = 1.0 / jnp.sqrt(total_sq / count + epsilon)
    unit = attention * inverse_rms[:, None, None]
    mean_grad = lax.psum(jnp.sum(unit * grad_in, axis=(1, 2)), "head") / count
    normed = (gain_b * unit).astype(jnp.bfloat16)
    d_attention = ((grad_in - unit * mean_grad[:, None, None]) * inverse_rms[:, None, None]).astype(
        jnp.bfloat16
    )
    d_scores = jnp.einsum("thd,shd->hts", d_attention, value, preferred_element_type=jnp.float32)
    d_weights = jnp.where(causal, d_scores, 0.0).astype(jnp.bfloat16)
    d_att_f = d_attention.astype(jnp.float32)
    grad_query = jnp.einsum("hts,shd->thd", d_weights, key, preferred_element_type=jnp.float32)
    grad_query = grad_query + jnp.einsum("thj,hij->thi", d_att_f, prefix, precision=high)
    block_grad = jnp.einsum("thi,thj->hij", query, d_attention, preferred_element_type=jnp.float32)
    suffix = entering(block_grad, "ctx", add_states, zero_state, True)
    grad_key = jnp.einsum("hts,thd->shd", d_weights, query, preferred_element_type=jnp.float32)
    grad_key = grad_key + jnp.einsum(
        "shj,hij->shi", value.astype(jnp.float32), suffix, precision=high
    )
    grad_value = jnp.einsum(
        "hts,thd->shd", weights, d_attention, preferred_element_type=jnp.float32
    )
    grad_value = grad_value + jnp.einsum(
        "shi,hij->shj", key.astype(jnp.float32), suffix, precision=high
    )
    key_value = jnp.stack((key2, softmax_values))
    blocks = [key_value]
    for offset in range(1, WINDOW_BLOCKS):
        blocks.append(from_behind(key_value, "ctx", offset))
    window = jnp.concatenate(blocks[::-1], axis=1)
    columns = lax.broadcasted_iota(jnp.int32, (block_rows, WINDOW_BLOCKS * block_rows), 1)
    query_ids = lax.broadcasted_iota(jnp.int32, (block_rows, WINDOW_BLOCKS * block_rows), 0)
    block_back = WINDOW_BLOCKS - 1 - columns // block_rows
    usable = (position - block_back >= 0) & ((block_back > 0) | (columns % block_rows <= query_ids))
    softmax_query = (query2.astype(jnp.float32) + normed.astype(jnp.float32)).astype(jnp.bfloat16)
    kv_heads = key2.shape[1]
    query_group_count = head_count // kv_heads
    query_groups = jnp.moveaxis(
        softmax_query.reshape(block_rows, kv_heads, query_group_count, head_width), 2, 0
    )

    def attend(query_part):
        logits = jnp.einsum(
            "tkd,skd->kts", query_part, window[0], preferred_element_type=jnp.float32
        ) * head_width ** (-0.5)
        logits = jnp.where(usable[None], logits, -1e30)
        row_max = jnp.max(logits, axis=-1, keepdims=True)
        exponent = jnp.exp(logits - row_max)
        probs = (exponent / jnp.sum(exponent, axis=-1, keepdims=True)).astype(jnp.bfloat16)
        return jnp.einsum("kts,skd->tkd", probs, window[1], preferred_element_type=jnp.float32)

    results = lax.map(attend, query_groups)
    attended = (
        jnp.moveaxis(results, 0, 2).reshape(block_rows, head_count, head_width).astype(jnp.bfloat16)
    )
    return (
        normed,
        grad_query.astype(jnp.bfloat16),
        grad_key.astype(jnp.bfloat16),
        grad_value.astype(jnp.bfloat16),
        attended,
    )


def solution(mesh):
    placed = (
        P("ctx", "head", None),
        P("ctx", "head", None),
        P("ctx", "head", None),
        P("head", None),
        P("ctx", "head", None),
        P("ctx", "head", None),
        P("ctx", "head", None),
        P("ctx", "head", None),
    )
    return jax.shard_map(
        local,
        mesh=mesh,
        in_specs=placed,
        out_specs=(
            P("ctx", "head", None),
            P("ctx", "head", None),
            P("ctx", "head", None),
            P("ctx", "head", None),
            P("ctx", "head", None),
        ),
        check_vma=False,
    )
```

profile of v0, /device:TPU:8, one launch (start us, length us, event | category | flops | bytes accessed | tf_op | source)
XLA Modules:
  0.0 462.0 jit_solution(15041282697065898238)
XLA Ops:
  8.4 2.6 fusion.22
  11.1 2.4 copy.76
  13.5 2.4 copy.90
  16.7 2.6 select_convert_fusion.1
  19.3 1.9 copy-done.1
  21.3 2.8 fusion.18
  24.1 129.3 %all-gather.5.cloned.1.call-done = f32[256,128,128]{2,1,0:T(8,128)} async-done(((f32[8,128,128]{2,1,0:T(8,128)}), f32[256,128,128]{2,1,0:T(8,128)}) %all-gather.5.cloned.1.call-update) | async-done | bytes 16777232 | tf_op jit(solution)/shard_map/all_gather | solution.py:17
  153.4 38.8 %while.40 = (s32[]{:T(128)}, f32[8,128,128]{2,1,0:T(8,128)S(1)}, s32[]{:T(128)}, f32[32,8,128,128]{3,2,1,0:T(8,128)}, s32[]{:T(128)}, /*index=5*/s32[]{:T(128)}) while((s32[]{:T(128)}, f32[8,128,128]{2,1,0:T(8,128)S(1)}, s32[]{:T(128)}, f32[32,8,128,128]{3,2,1,0:T(8,128)}, s32[]{:T(128)}, /*index=5*/s32[]{:T(128)}) %tuple.108), condition=%wide.region_1.2_spmd.clone, body=%wide.region_0.1_spmd.clone.sunk | while | flops 393220 | bytes 1572965 | solution.py:27
  192.2 4.1 multiply_reduce_fusion.1
  196.3 14.1 %psum.14 = f32[512]{0:T(512)S(1)} all-reduce(f32[512]{0:T(512)S(1)} %get-tuple-element.345), channel_id=1, replica_groups=mesh['ctx'=32,'head'=8] {'head'}, use_global_device_ids=true, to_apply=%region_3.4 | all-reduce | flops 512 | bytes 4096 | tf_op jit(solution)/shard_map/psum | solution.py:64
  210.4 2.3 multiply_reduce_fusion
  212.7 12.4 %psum.15 = f32[512]{0:T(512)S(1)} all-reduce(f32[512]{0:T(512)S(1)} %multiply_reduce_fusion), channel_id=1, replica_groups=mesh['ctx'=32,'head'=8] {'head'}, use_global_device_ids=true, to_apply=%region_5.6 | all-reduce | flops 512 | bytes 4096 | tf_op jit(solution)/shard_map/psum | solution.py:67
  225.2 4.4 fusion.17
  231.8 1.9 collective-permute-start.2
  233.7 5.4 %collective-permute-start.1 = (bf16[2,512,1,128]{3,1,2,0:T(8,128)(2,1)}, bf16[2,512,1,128]{3,1,2,0:T(8,128)(2,1)}, u32[]{:S(2)}, u32[]{:S(2)}) collective-permute-start(bf16[2,512,1,128]{3,1,2,0:T(8,128)(2,1)} %pad_maximum_fusion), channel_id=1, source_target_pairs={{0,16},{8,24},{16,32},{24,40},{32,48},{40,56},{48,64},{56,72},{64,... | collective-permute-start | bytes 786440 | tf_op jit(solution)/shard_map/ppermute | solution.py:33
  239.2 3.6 collective-permute-start
  242.9 5.3 %collective-permute-done.2 = bf16[2,512,1,128]{3,1,2,0:T(8,128)(2,1)} collective-permute-done((bf16[2,512,1,128]{3,1,2,0:T(8,128)(2,1)}, bf16[2,512,1,128]{3,1,2,0:T(8,128)(2,1)}, u32[]{:S(2)}, u32[]{:S(2)}) %collective-permute-start.2) | collective-permute-done | bytes 262176 | tf_op jit(solution)/shard_map/ppermute | solution.py:33
  248.2 15.9 %collective-permute-done.1 = bf16[2,512,1,128]{3,1,2,0:T(8,128)(2,1)} collective-permute-done((bf16[2,512,1,128]{3,1,2,0:T(8,128)(2,1)}, bf16[2,512,1,128]{3,1,2,0:T(8,128)(2,1)}, u32[]{:S(2)}, u32[]{:S(2)}) %collective-permute-start.1) | collective-permute-done | bytes 262176 | tf_op jit(solution)/shard_map/ppermute | solution.py:33
  264.1 20.4 %collective-permute-done = bf16[2,512,1,128]{3,1,2,0:T(8,128)(2,1)} collective-permute-done((bf16[2,512,1,128]{3,1,2,0:T(8,128)(2,1)}, bf16[2,512,1,128]{3,1,2,0:T(8,128)(2,1)}, u32[]{:S(2)}, u32[]{:S(2)}) %collective-permute-start) | collective-permute-done | bytes 262176 | tf_op jit(solution)/shard_map/ppermute | solution.py:33
  284.5 2.1 maximum_maximum_fusion
  286.6 2.4 copy.93
  289.1 2.5 select_convert_fusion
  291.6 1.2 fusion.26
  292.9 1.2 fusion.15
  294.1 1.6 copy.94
  295.8 2.1 fusion.41
  297.9 2.8 fusion.30
  300.7 93.5 %while.39 = (s32[]{:T(128)}, bf16[8,512,1,128]{3,0,1,2:T(8,128)(2,1)}, bf16[8,512,1,128]{1,3,0,2:T(8,128)(2,1)}, bf16[2,2048,1,128]{3,1,2,0:T(8,128)(2,1)S(1)}, ...) while((s32[]{:T(128)}, ...), condition=%wide.region_11.12_spmd.clone, body=%wide.region_8.11_spmd.clone.sunk | while | flops 554695680 | bytes 14596749 | solution.py:115
  300.7 2.4 fusion.59
  304.7 7.8 %dynamic_update_slice.6 = bf16[8,512,1,128]{3,0,1,2:T(8,128)(2,1)} dynamic-update-slice(bf16[8,512,1,128]{3,0,1,2:T(8,128)(2,1)} %get-tuple-element.524, f32[1,512,1,128]{3,0,1,2:T(1,128)S(1)} %bitcast.85, s32[]{:T(128)S(6)} %copy.150, s32[]{:T(128)} %constant.105.clone.1..sunk, s32[]{:T(128)} %constant.105.clone.1..sunk, s32[]{:T(128)} %constant.105.clone.1..sunk) | dynamic-update-slice | bytes 524292 | tf_op jit(solution)/shard_map/while/body/jit(dynamic_update_index_in_dim)/dynamic_update_slice | solution.py:115
  312.5 2.3 fusion.59
  316.4 7.8 %dynamic_update_slice.6 = bf16[8,512,1,128]{3,0,1,2:T(8,128)(2,1)} dynamic-update-slice(bf16[8,512,1,128]{3,0,1,2:T(8,128)(2,1)} %get-tuple-element.524, f32[1,512,1,128]{3,0,1,2:T(1,128)S(1)} %bitcast.85, s32[]{:T(128)S(6)} %copy.150, s32[]{:T(128)} %constant.105.clone.1..sunk, s32[]{:T(128)} %constant.105.clone.1..sunk, s32[]{:T(128)} %constant.105.clone.1..sunk) | dynamic-update-slice | bytes 524292 | tf_op jit(solution)/shard_map/while/body/jit(dynamic_update_index_in_dim)/dynamic_update_slice | solution.py:115
  324.1 2.3 fusion.59
  328.1 7.8 %dynamic_update_slice.6 = bf16[8,512,1,128]{3,0,1,2:T(8,128)(2,1)} dynamic-update-slice(bf16[8,512,1,128]{3,0,1,2:T(8,128)(2,1)} %get-tuple-element.524, f32[1,512,1,128]{3,0,1,2:T(1,128)S(1)} %bitcast.85, s32[]{:T(128)S(6)} %copy.150, s32[]{:T(128)} %constant.105.clone.1..sunk, s32[]{:T(128)} %constant.105.clone.1..sunk, s32[]{:T(128)} %constant.105.clone.1..sunk) | dynamic-update-slice | bytes 524292 | tf_op jit(solution)/shard_map/while/body/jit(dynamic_update_index_in_dim)/dynamic_update_slice | solution.py:115
  335.8 2.3 fusion.59
  339.7 7.8 %dynamic_update_slice.6 = bf16[8,512,1,128]{3,0,1,2:T(8,128)(2,1)} dynamic-update-slice(bf16[8,512,1,128]{3,0,1,2:T(8,128)(2,1)} %get-tuple-element.524, f32[1,512,1,128]{3,0,1,2:T(1,128)S(1)} %bitcast.85, s32[]{:T(128)S(6)} %copy.150, s32[]{:T(128)} %constant.105.clone.1..sunk, s32[]{:T(128)} %constant.105.clone.1..sunk, s32[]{:T(128)} %constant.105.clone.1..sunk) | dynamic-update-slice | bytes 524292 | tf_op jit(solution)/shard_map/while/body/jit(dynamic_update_index_in_dim)/dynamic_update_slice | solution.py:115
  347.5 2.3 fusion.59
  351.4 7.8 %dynamic_update_slice.6 = bf16[8,512,1,128]{3,0,1,2:T(8,128)(2,1)} dynamic-update-slice(bf16[8,512,1,128]{3,0,1,2:T(8,128)(2,1)} %get-tuple-element.524, f32[1,512,1,128]{3,0,1,2:T(1,128)S(1)} %bitcast.85, s32[]{:T(128)S(6)} %copy.150, s32[]{:T(128)} %constant.105.clone.1..sunk, s32[]{:T(128)} %constant.105.clone.1..sunk, s32[]{:T(128)} %constant.105.clone.1..sunk) | dynamic-update-slice | bytes 524292 | tf_op jit(solution)/shard_map/while/body/jit(dynamic_update_index_in_dim)/dynamic_update_slice | solution.py:115
  359.2 2.3 fusion.59
  363.1 7.8 %dynamic_update_slice.6 = bf16[8,512,1,128]{3,0,1,2:T(8,128)(2,1)} dynamic-update-slice(bf16[8,512,1,128]{3,0,1,2:T(8,128)(2,1)} %get-tuple-element.524, f32[1,512,1,128]{3,0,1,2:T(1,128)S(1)} %bitcast.85, s32[]{:T(128)S(6)} %copy.150, s32[]{:T(128)} %constant.105.clone.1..sunk, s32[]{:T(128)} %constant.105.clone.1..sunk, s32[]{:T(128)} %constant.105.clone.1..sunk) | dynamic-update-slice | bytes 524292 | tf_op jit(solution)/shard_map/while/body/jit(dynamic_update_index_in_dim)/dynamic_update_slice | solution.py:115
  370.9 2.3 fusion.59
  374.8 7.8 %dynamic_update_slice.6 = bf16[8,512,1,128]{3,0,1,2:T(8,128)(2,1)} dynamic-update-slice(bf16[8,512,1,128]{3,0,1,2:T(8,128)(2,1)} %get-tuple-element.524, f32[1,512,1,128]{3,0,1,2:T(1,128)S(1)} %bitcast.85, s32[]{:T(128)S(6)} %copy.150, s32[]{:T(128)} %constant.105.clone.1..sunk, s32[]{:T(128)} %constant.105.clone.1..sunk, s32[]{:T(128)} %constant.105.clone.1..sunk) | dynamic-update-slice | bytes 524292 | tf_op jit(solution)/shard_map/while/body/jit(dynamic_update_index_in_dim)/dynamic_update_slice | solution.py:115
  382.6 2.3 fusion.59
  386.5 7.8 %dynamic_update_slice.6 = bf16[8,512,1,128]{3,0,1,2:T(8,128)(2,1)} dynamic-update-slice(bf16[8,512,1,128]{3,0,1,2:T(8,128)(2,1)} %get-tuple-element.524, f32[1,512,1,128]{3,0,1,2:T(1,128)S(1)} %bitcast.85, s32[]{:T(128)S(6)} %copy.150, s32[]{:T(128)} %constant.105.clone.1..sunk, s32[]{:T(128)} %constant.105.clone.1..sunk, s32[]{:T(128)} %constant.105.clone.1..sunk) | dynamic-update-slice | bytes 524292 | tf_op jit(solution)/shard_map/while/body/jit(dynamic_update_index_in_dim)/dynamic_update_slice | solution.py:115
  394.2 11.6 %rev.3 = f32[32,8,128,128]{3,2,1,0:T(8,128)} reverse(f32[32,8,128,128]{3,2,1,0:T(8,128)} %bitcast.84), dimensions={0} | reverse | bytes 33554432 | tf_op jit(solution)/shard_map/rev | solution.py:19
  405.9 38.9 %while.41 = (s32[]{:T(128)}, f32[8,128,128]{2,1,0:T(8,128)S(1)}, s32[]{:T(128)}, f32[32,8,128,128]{3,2,1,0:T(8,128)}, s32[]{:T(128)}, /*index=5*/s32[]{:T(128)}) while((s32[]{:T(128)}, f32[8,128,128]{2,1,0:T(8,128)S(1)}, s32[]{:T(128)}, f32[32,8,128,128]{3,2,1,0:T(8,128)}, s32[]{:T(128)}, /*index=5*/s32[]{:T(128)}) %tuple.97), condition=%wide.region_7.8_spmd.clone, body=%wide.region_6.7_spmd.clone.sunk | while | flops 393220 | bytes 1572965 | solution.py:27
  405.9 1.3 add_select_fusion.5
  407.2 1.2 add_select_fusion.5
  408.5 1.2 add_select_fusion.5
  409.7 1.2 add_select_fusion.5
  413.5 1.2 add_select_fusion.5
  414.7 1.2 add_select_fusion.5
  419.8 1.2 add_select_fusion.5
  421.0 1.2 add_select_fusion.5
  426.0 1.2 add_select_fusion.5
  427.3 1.2 add_select_fusion.5
  432.3 1.2 add_select_fusion.5
  437.3 1.2 add_select_fusion.5
  438.6 1.2 add_select_fusion.5
  443.6 1.2 add_select_fusion.5
  444.8 3.6 fusion.16
  448.5 2.4 copy.96
  450.9 2.6 fusion.14
  453.6 1.6 copy.95
  (106 shorter events, 76.0 us)
Async XLA Ops:
  7.2 1.2 copy-start
  7.2 9.5 %copy-start.3 = (bf16[512,8,128]{2,1,0:T(8,128)(2,1)S(1)}, bf16[512,8,128]{2,1,0:T(8,128)(2,1)}, u32[]{:S(2)}) copy-start(bf16[512,8,128]{2,1,0:T(8,128)(2,1)} %param.14) | copy-start | bytes 3145732
  7.2 146.2 %all-gather.5.cloned.1.call-start = ((), (), s32[]{:S(2)}) async-start(), calls=%async_computation | async-start | bytes 17301504 | tf_op jit(solution)/shard_map/all_gather | solution.py:17
  11.0 383.2 %all-gather.7.cloned.1.call-start = ((), (), s32[]{:S(2)}) async-start(), calls=%async_computation.1 | async-start | bytes 17301504 | tf_op jit(solution)/shard_map/all_gather | solution.py:17
  16.0 0.7 copy-start.11
  19.3 1.9 copy-start.1
  192.2 18.2 %copy-start.12 = (f32[8,128]{1,0:T(8,128)S(1)}, f32[8,128]{1,0:T(8,128)}, u32[]{:S(2)}) copy-start(f32[8,128]{1,0:T(8,128)} %param.17) | copy-start | bytes 12292
  225.1 4.4 copy-start.4
  225.1 5.9 %copy-start.9 = (bf16[512,1,128]{2,0,1:T(8,128)(2,1)S(1)}, bf16[512,1,128]{2,0,1:T(8,128)(2,1)}, u32[]{:S(2)}) copy-start(bf16[512,1,128]{2,0,1:T(8,128)(2,1)} %param.21) | copy-start | bytes 393220
  225.2 5.9 %copy-start.10 = (bf16[512,1,128]{2,0,1:T(8,128)(2,1)S(1)}, bf16[512,1,128]{2,0,1:T(8,128)(2,1)}, u32[]{:S(2)}) copy-start(bf16[512,1,128]{2,0,1:T(8,128)(2,1)} %param.20) | copy-start | bytes 393220
  231.8 16.4 %collective-permute-start.2 = (bf16[2,512,1,128]{3,1,2,0:T(8,128)(2,1)}, bf16[2,512,1,128]{3,1,2,0:T(8,128)(2,1)}, u32[]{:S(2)}, u32[]{:S(2)}) collective-permute-start(bf16[2,512,1,128]{3,1,2,0:T(8,128)(2,1)} %pad_maximum_fusion), channel_id=1, source_target_pairs={{0,8},{8,16},{16,24},{24,32},{32,40},{40,48},{48,56},{56,64},{64,7... | collective-permute-start | bytes 786440 | tf_op jit(solution)/shard_map/ppermute | solution.py:33
  233.7 30.4 %collective-permute-start.1 = (bf16[2,512,1,128]{3,1,2,0:T(8,128)(2,1)}, bf16[2,512,1,128]{3,1,2,0:T(8,128)(2,1)}, u32[]{:S(2)}, u32[]{:S(2)}) collective-permute-start(bf16[2,512,1,128]{3,1,2,0:T(8,128)(2,1)} %pad_maximum_fusion), channel_id=1, source_target_pairs={{0,16},{8,24},{16,32},{24,40},{32,48},{40,56},{48,64},{56,72},{64,... | collective-permute-start | bytes 786440 | tf_op jit(solution)/shard_map/ppermute | solution.py:33
  239.2 45.3 %collective-permute-start = (bf16[2,512,1,128]{3,1,2,0:T(8,128)(2,1)}, bf16[2,512,1,128]{3,1,2,0:T(8,128)(2,1)}, u32[]{:S(2)}, u32[]{:S(2)}) collective-permute-start(bf16[2,512,1,128]{3,1,2,0:T(8,128)(2,1)} %pad_maximum_fusion), channel_id=1, source_target_pairs={{0,24},{8,32},{16,40},{24,48},{32,56},{40,64},{48,72},{56,80},{64,... | collective-permute-start | bytes 786440 | tf_op jit(solution)/shard_map/ppermute | solution.py:33
  289.1 2.5 copy-start.6
  292.8 2.9 copy-start.2
  295.8 2.1 copy-start.5
  297.9 2.8 copy-start.8
  405.9 38.9 %copy-start.7 = (bf16[512,8,128]{2,1,0:T(8,128)(2,1)S(1)}, bf16[512,8,128]{2,1,0:T(8,128)(2,1)}, u32[]{:S(2)}) copy-start(bf16[512,8,128]{2,1,0:T(8,128)(2,1)} %param.15) | copy-start | bytes 3145732
Sparse Core Ops, SparseCore 0:
  11.2 142.1 all-gather.4
  231.2 155.2 all-gather.6
where the time goes:
time: 467 us; the launch traced here: 462 us
  waiting for transfers between devices  171 us (37%)
  local copies, waits for them, and re-layouts  91.7 us (20%)
  other arithmetic  91.6 us (20%)
  matrix products  54.4 us (12%)
  blocking collectives  26.5 us (6%)
  between operations  14.3 us (3%)
  starting transfers between devices  11.1 us (2%)
    all_gather x2, waiting for transfers between devices, entering(): pieces = lax.all_gather(value, axis)  129 us
    select_n x62, other arithmetic, hop(): return jnp.where(position < mine, longer, so_far)  76.2 us
    dynamic_update_slice x8, local copies, waits for them, and re-layouts, local(): results = lax.map(attend, query_groups)  62.2 us
    ppermute x3, waiting for transfers between devices, from_behind(): return lax.ppermute(shard, axis, pairs)  41.6 us
    dot_general x8, matrix products, attend(): jnp.einsum('tkd,skd->kts', query_part, window[0], preferred_element_type=...  18.5 us
    unnamed x32, local copies, waits for them, and re-layouts  16.8 us
    psum x1, blocking collectives, local(): total_sq = lax.psum(local_squares, 'head')  14.1 us
    psum x1, blocking collectives, local(): mean_grad = lax.psum(jnp.sum(unit * grad_in, axis=(1, 2)), 'head') / count  12.4 us
  transfers between devices with their start and end apart: 5, of which 4 were waited for; matrix products, arithmetic and copies ran while one was open for 26% of the time, Pallas kernels for 0%

commit v1 on v0

v1 whole, which is shorter than its diff:
```python
import functools
import jax
import jax.numpy as jnp
from jax import lax
from jax.experimental import pallas as pl
from jax.experimental.pallas import tpu as pltpu
from jax.sharding import Mesh, PartitionSpec as P

ATTN_HEADS = 64
HEAD_WIDTH = 128
WINDOW_BLOCKS = 4
CHANNELS = ATTN_HEADS * HEAD_WIDTH
EPSILON = 1e-06
LOG2E = 1.4426950408889634

f32 = jnp.float32
bf16 = jnp.bfloat16
MIB = 1 << 20
HEADS = ("x", "core")
CTX = ("y", "z")


def nn(a, b, precision=None):
    return lax.dot_general(
        a, b, (((1,), (0,)), ((), ())), precision=precision, preferred_element_type=f32
    )


def nt(a, b, precision=None):
    return lax.dot_general(
        a, b, (((1,), (1,)), ((), ())), precision=precision, preferred_element_type=f32
    )


def tn(a, b, precision=None):
    return lax.dot_general(
        a, b, (((0,), (0,)), ((), ())), precision=precision, preferred_element_type=f32
    )


def call(kernel, out_shapes, args, scratch=(), flops=0, smem_first=False, vmem=48):
    specs = [pl.BlockSpec(memory_space=pltpu.VMEM) for _ in args]
    if smem_first:
        specs[0] = pl.BlockSpec(memory_space=pltpu.SMEM)
    moved = sum(a.size * a.dtype.itemsize for a in (*args, *out_shapes))
    return pl.pallas_call(
        kernel,
        out_shape=out_shapes,
        in_specs=specs,
        out_specs=[pl.BlockSpec(memory_space=pltpu.VMEM) for _ in out_shapes],
        scratch_shapes=list(scratch),
        compiler_params=pltpu.CompilerParams(vmem_limit_bytes=vmem * MIB),
        cost_estimate=pl.CostEstimate(flops=flops, bytes_accessed=moved, transcendentals=0),
    )(*args)


def shape(dims, dtype):
    return jax.ShapeDtypeStruct(dims, dtype)


def state_kernel(k_ref, v_ref, kh_ref, vh_ref, st_ref, ks, vs):
    tokens, heads, width = k_ref.shape
    ks[...] = k_ref[...].astype(f32).reshape(tokens * heads, width)
    vs[...] = v_ref[...].astype(f32).reshape(tokens * heads, width)
    for h in range(heads):
        kh = ks[pl.ds(h, tokens, stride=heads), :].astype(bf16)
        vh = vs[pl.ds(h, tokens, stride=heads), :].astype(bf16)
        kh_ref[h] = kh
        vh_ref[h] = vh
        st_ref[h] = tn(kh, vh).astype(bf16)


def causal_below(rows):
    r = lax.broadcasted_iota(jnp.int32, (rows, rows), 0)
    c = lax.broadcasted_iota(jnp.int32, (rows, rows), 1)
    return c <= r


def local_kernel(q_ref, c_ref, gain_ref, kh_ref, vh_ref, qh_ref, gh_ref, loc_ref, qs, cs):
    tokens, heads, width = q_ref.shape
    half = tokens // 2
    qs[...] = q_ref[...].astype(f32).reshape(tokens * heads, width)
    cs[...] = (c_ref[...].astype(f32) * gain_ref[...][None]).reshape(tokens * heads, width)
    causal = causal_below(half)
    for h in range(heads):
        qh = qs[pl.ds(h, tokens, stride=heads), :].astype(bf16)
        qh_ref[h] = qh
        gh_ref[h] = cs[pl.ds(h, tokens, stride=heads), :]
        kh = kh_ref[h]
        vh = vh_ref[h]
        w0 = jnp.where(causal, nt(qh[:half], kh[:half]), 0.0).astype(bf16)
        w10 = nt(qh[half:], kh[:half]).astype(bf16)
        w11 = jnp.where(causal, nt(qh[half:], kh[half:]), 0.0).astype(bf16)
        loc_ref[h, :half] = nn(w0, vh[:half])
        loc_ref[h, half:] = nn(w10, vh[:half]) + nn(w11, vh[half:])


def attention_kernel(loc_ref, qh_ref, gh_ref, pre_ref, att_ref, part_ref):
    heads, tokens, width = loc_ref.shape
    squares = jnp.zeros((tokens, width), f32)
    inner = jnp.zeros((tokens, width), f32)
    for h in range(heads):
        att = loc_ref[h] + nn(qh_ref[h], pre_ref[h])
        att_ref[h] = att
        squares = squares + att * att
        inner = inner + att * gh_ref[h]
    ones = jnp.ones((8, width), f32)
    part_ref[0:1] = nt(ones, squares, lax.Precision.HIGHEST)[0:1]
    part_ref[1:2] = nt(ones, inner, lax.Precision.HIGHEST)[0:1]


def row_scales(g_ref):
    ones = jnp.ones((g_ref.shape[0], HEAD_WIDTH), f32)
    squares = tn(g_ref[:, 0, :], ones, lax.Precision.HIGHEST)
    inner = tn(g_ref[:, 1, :], ones, lax.Precision.HIGHEST)
    inverse = 1.0 / jnp.sqrt(squares / CHANNELS + EPSILON)
    return inverse, inverse * inner / CHANNELS


def backward_kernel(g_ref, att_ref, gh_ref, qh_ref, da_ref, bg_ref, inv_ref):
    heads, tokens, width = att_ref.shape
    inverse, mean = row_scales(g_ref)
    inv_ref[...] = inverse
    scaled = inverse * mean
    for h in range(heads):
        da = ((gh_ref[h] - att_ref[h] * scaled) * inverse).astype(bf16)
        da_ref[h] = da
        bg_ref[h] = tn(qh_ref[h], da).astype(bf16)


def softmax_kernel(
    pos_ref, att_ref, inv_ref, gain_ref, q2_ref, kv0_ref, kv1_ref, kv2_ref, kv3_ref,
    norm_ref, out_ref, scratch,
):
    heads, tokens, width = att_ref.shape
    inverse = inv_ref[...]
    for h in range(heads):
        scratch[pl.ds(h, tokens, stride=heads), :] = (
            gain_ref[h : h + 1, :] * (att_ref[h] * inverse)
        )
    normed = scratch[...].astype(bf16)
    norm_ref[...] = normed.reshape(tokens, heads, width)

    rows = 256
    groups = 4
    chunks = tokens * heads // rows
    per_group = chunks // groups
    scale = LOG2E * HEAD_WIDTH ** (-0.5)
    ones = jnp.ones((tokens, width), bf16)
    token_chunk = rows // heads
    blocks = (kv0_ref, kv1_ref, kv2_ref, kv3_ref)

    def run(count):
        for group in range(groups):
            limit = tokens // groups * (group + 1)

            def body(step, carry):
                chunk = group * per_group + step
                first = pl.multiple_of(chunk * rows, rows)
                t0 = pl.multiple_of(chunk * token_chunk, token_chunk)
                n = scratch[pl.ds(first, rows), :].astype(bf16).astype(f32)
                q2 = q2_ref[pl.ds(t0, token_chunk)].astype(f32).reshape(rows, width)
                q = (q2 + n).astype(bf16)
                row_token = t0 + lax.broadcasted_iota(jnp.int32, (rows, limit), 0) // heads
                column = lax.broadcasted_iota(jnp.int32, (rows, limit), 1)
                scores = [
                    jnp.where(column <= row_token, nt(q, blocks[0][0, :limit]), -1e30)
                ]
                for b in range(1, count):
                    scores.append(nt(q, blocks[b][0]))
                top = jnp.max(scores[0], axis=1, keepdims=True)
                for s in scores[1:]:
                    top = jnp.maximum(top, jnp.max(s, axis=1, keepdims=True))
                top = top * scale
                total = None
                for b, s in enumerate(scores):
                    p = jnp.exp2(s * scale - top).astype(bf16)
                    n_keys = s.shape[1]
                    v = jnp.concatenate([blocks[b][1, :n_keys], ones[:n_keys]], axis=1)
                    o = nn(p, v)
                    total = o if total is None else total + o
                result = total[:, :width] / total[:, width:]
                out_ref[pl.ds(t0, token_chunk)] = result.astype(bf16).reshape(
                    token_chunk, heads, width
                )
                return carry

            lax.fori_loop(0, per_group, body, 0)

    have = pos_ref[0]
    for count in range(1, WINDOW_BLOCKS + 1):
        pl.when(have == count - 1)(functools.partial(run, count))


def gradient_kernel(
    qh_ref, kh_ref, vh_ref, da_ref, pre_ref, suf_ref, gq_ref, gk_ref, gv_ref, qs, ks, vs
):
    heads, tokens, width = qh_ref.shape
    half = tokens // 2
    below = causal_below(half)
    r = lax.broadcasted_iota(jnp.int32, (half, half), 0)
    c = lax.broadcasted_iota(jnp.int32, (half, half), 1)
    above = r <= c
    lo, hi = slice(0, half), slice(half, tokens)

    def low(x):
        return jnp.where(below, x, 0.0).astype(bf16)

    def up(x):
        return jnp.where(above, x, 0.0).astype(bf16)

    for h in range(heads):
        q, k, v, da = qh_ref[h], kh_ref[h], vh_ref[h], da_ref[h]
        pre, suf = pre_ref[h], suf_ref[h]
        d00 = low(nt(da[lo], v[lo]))
        d10 = nt(da[hi], v[lo]).astype(bf16)
        d11 = low(nt(da[hi], v[hi]))
        gq = nt(da, pre)
        gq0 = gq[lo] + nn(d00, k[lo])
        gq1 = gq[hi] + nn(d10, k[lo]) + nn(d11, k[hi])
        t00 = up(nt(v[lo], da[lo]))
        t01 = nt(v[lo], da[hi]).astype(bf16)
        t11 = up(nt(v[hi], da[hi]))
        gk = nt(v, suf)
        gk0 = gk[lo] + nn(t00, q[lo]) + nn(t01, q[hi])
        gk1 = gk[hi] + nn(t11, q[hi])
        w00 = up(nt(k[lo], q[lo]))
        w01 = nt(k[lo], q[hi]).astype(bf16)
        w11 = up(nt(k[hi], q[hi]))
        gv = nn(k, suf)
        gv0 = gv[lo] + nn(w00, da[lo]) + nn(w01, da[hi])
        gv1 = gv[hi] + nn(w11, da[hi])
        for ref, first, second in ((qs, gq0, gq1), (ks, gk0, gk1), (vs, gv0, gv1)):
            ref[pl.ds(h, half, stride=heads), :] = first
            ref[pl.ds(half * heads + h, half, stride=heads), :] = second
    for ref, out in ((qs, gq_ref), (ks, gk_ref), (vs, gv_ref)):
        out[...] = ref[...].astype(bf16).reshape(tokens, heads, width)


def scan_kernel(back, recv_ref, t1_ref, t2_ref, t3_ref, out_ref):
    count = recv_ref.shape[0]
    running = t1_ref[...].astype(f32) + t2_ref[...].astype(f32) + t3_ref[...].astype(f32)
    order = range(count - 1, -1, -1) if back else range(count)
    for i in order:
        out_ref[i] = running.astype(bf16)
        running = running + recv_ref[i].astype(f32)


def total_kernel(recv_ref, out_ref):
    total = recv_ref[0].astype(f32)
    for i in range(1, recv_ref.shape[0]):
        total = total + recv_ref[i].astype(f32)
    out_ref[...] = total.astype(bf16)


def exclusive(states, back):
    pieces = lax.all_to_all(states, "z", 0, 0, tiled=True)
    (total,) = call(total_kernel, [shape(states.shape[1:], bf16)], [pieces])
    rows = lax.axis_size("y")
    others = []
    for d in range(1, 4):
        pairs = [(i + d, i) if back else (i, i + d) for i in range(rows - d)]
        others.append(lax.ppermute(total, "y", pairs))
    (scanned,) = call(
        functools.partial(scan_kernel, back), [shape(pieces.shape, bf16)], [pieces, *others]
    )
    return lax.all_to_all(scanned, "z", 0, 0, tiled=True)


def local(query, key, value, gain, cotangent, query2, key2, softmax_values):
    tokens, heads, width = query.shape
    position = lax.axis_index(CTX)
    flat = (tokens * heads, width)
    head_major = (heads, tokens, width)
    square = (heads, width, width)
    unit = 2 * tokens * tokens * width * heads

    own = jnp.stack((key2[:, 0], softmax_values[:, 0]))
    ring = lax.axis_size(CTX)
    windows = [own]
    for _ in range(1, WINDOW_BLOCKS):
        windows.append(
            lax.ppermute(windows[-1], CTX, [(i, i + 1) for i in range(ring - 1)])
        )

    kh, vh, states = call(
        state_kernel,
        [shape(head_major, bf16), shape(head_major, bf16), shape(square, bf16)],
        [key, value],
        [pltpu.VMEM(flat, f32), pltpu.VMEM(flat, f32)],
        unit // 4,
    )
    prefix = exclusive(states, False)
    qh, gh, loc = call(
        local_kernel,
        [shape(head_major, bf16), shape(head_major, f32), shape(head_major, f32)],
        [query, cotangent, gain, kh, vh],
        [pltpu.VMEM(flat, f32), pltpu.VMEM(flat, f32)],
        2 * unit,
    )
    att, part = call(
        attention_kernel,
        [shape(head_major, f32), shape((2, tokens), f32)],
        [loc, qh, gh, prefix],
        (),
        unit // 4,
    )
    gathered = lax.all_gather(part, HEADS)
    da, block_grad, inverse = call(
        backward_kernel,
        [shape(head_major, bf16), shape(square, bf16), shape((tokens, width), f32)],
        [gathered, att, gh, qh],
        (),
        unit // 4,
    )
    suffix = exclusive(block_grad, True)
    have = jnp.minimum(position, WINDOW_BLOCKS - 1).astype(jnp.int32).reshape(1)
    normed, attended = call(
        softmax_kernel,
        [shape(query.shape, bf16), shape(query.shape, bf16)],
        [have, att, inverse, gain, query2, *windows],
        [pltpu.VMEM(flat, f32)],
        8 * unit,
        smem_first=True,
    )
    gq, gk, gv = call(
        gradient_kernel,
        [shape(query.shape, bf16)] * 3,
        [qh, kh, vh, da, prefix, suffix],
        [pltpu.VMEM(flat, f32)] * 3,
        6 * unit,
    )
    return normed, gq, gk, gv, attended


def solution(mesh):
    sizes = (4, 8, 4, 2)
    fine = Mesh(mesh.devices.reshape(sizes), ("y", "z", "x", "core"))
    tokens = P(CTX, HEADS, None)
    return jax.shard_map(
        local,
        mesh=fine,
        in_specs=(tokens, tokens, tokens, P(HEADS, None), tokens, tokens, tokens, tokens),
        out_specs=(tokens,) * 5,
        check_vma=False,
    )
```

time: 467 us -> 157 us (0.34)
  waiting for transfers between devices: 171 us -> 20.8 us
  other arithmetic: 91.6 us -> 0.72 us
  local copies, waits for them, and re-layouts: 91.7 us -> 17.6 us
  matrix products: 54.4 us -> 0 us
  Pallas kernels: 0 us -> 45 us
  starting transfers between devices: 11.1 us -> 36.3 us
  between operations: 14.3 us -> 0.89 us
  blocking collectives: 26.5 us -> 33.3 us
    all_gather x2 -> x0, waiting for transfers between devices: 129 us -> none  [entering(): pieces = lax.all_gather(value, axis)]
    select_n x62 -> x0, other arithmetic: 76.2 us -> none  [hop(): return jnp.where(position < mine, longer, so_far)]
    dynamic_update_slice x8 -> x0, local copies, waits for them, and re-layouts: 62.2 us -> none  [local(): results = lax.map(attend, query_groups)]
    dot_general x28 -> x0, matrix products: 54.4 us -> none  [the longest x8 18.5 us: attend(): jnp.einsum('tkd,skd->kts', query_part, window[0], preferred_element_type=...]
    pallas_call x0 -> x10, Pallas kernels: none -> 45 us  [call(): pl.pallas_call(kernel, out_shape=out_shapes, in_specs=specs, out_specs=[p...]
    psum x2 -> x0, blocking collectives: 26.5 us -> none  [the longest x1 14.1 us: local(): total_sq = lax.psum(local_squares, 'head')]
    ppermute x3 -> x9, waiting for transfers between devices: 41.6 us -> 20.4 us  [the longest x3 14.2 us: local(): lax.ppermute(windows[-1], CTX, [(i, i + 1) for i in range(ring - 1)])]
    all_to_all x0 -> x1, blocking collectives: none -> 20.1 us  [exclusive(): pieces = lax.all_to_all(states, 'z', 0, 0, tiled=True)]
  transfers between devices with their start and end apart: 5 -> 12, of which waited for: 4 -> 5; matrix products, arithmetic and copies ran while one was open for 26% -> 0% of each run, Pallas kernels for 0% -> 22%
where the time goes in v1:
time: 157 us; the launch traced here: 155 us
  Pallas kernels  45 us (29%)
  starting transfers between devices  36.3 us (23%)
  blocking collectives  33.3 us (21%)
  waiting for transfers between devices  20.8 us (13%)
  local copies, waits for them, and re-layouts  17.6 us (11%)
    pallas_call x10, Pallas kernels, call(): pl.pallas_call(kernel, out_shape=out_shapes, in_specs=specs, out_specs=[p...  45 us
    all_to_all x1, blocking collectives, exclusive(): pieces = lax.all_to_all(states, 'z', 0, 0, tiled=True)  20.1 us
    unnamed x46, local copies, waits for them, and re-layouts  17.6 us
    ppermute x3, waiting for transfers between devices, local(): lax.ppermute(windows[-1], CTX, [(i, i + 1) for i in range(ring - 1)])  14.2 us
    all_gather x1, blocking collectives, local(): gathered = lax.all_gather(part, HEADS)  13.2 us
    ppermute x6, starting transfers between devices, exclusive(): others.append(lax.ppermute(total, 'y', pairs))  10.3 us
    all_to_all x2, starting transfers between devices, exclusive(): return lax.all_to_all(scanned, 'z', 0, 0, tiled=True)  9.66 us
    ppermute x3, starting transfers between devices, local(): lax.ppermute(windows[-1], CTX, [(i, i + 1) for i in range(ring - 1)])  9.63 us
  transfers between devices with their start and end apart: 12, of which 5 were waited for; matrix products, arithmetic and copies ran while one was open for 0% of the time, Pallas kernels for 22%

profile of v1, /device:TPU:8, one launch (start us, length us, event | category | flops | bytes accessed | tf_op | source)
XLA Modules:
  0.0 154.6 jit_solution(8662781206004220619)
XLA Ops:
  0.6 0.0 copy-start.2
  0.6 0.0 copy-start.1
  0.7 0.0 copy-start.9
  0.7 1.4 copy-done.9
  2.0 1.2 copy-done.10
  3.3 1.3 shard_map.119
  4.5 0.0 copy-start.3
  4.5 1.0 copy-done.3
  5.5 1.0 copy-done.6
  6.5 20.1 %all_to_all.20.recv_ref = bf16[8,128,128]{2,1,0:T(8,128)(2,1)S(1)} all-to-all(bf16[8,128,128]{2,1,0:T(8,128)(2,1)S(1)} %get-tuple-element.26), channel_id=1, replica_groups=mesh['y'=4,'z'=8,'x'=4,'core'=2] {'z'}, dimensions={0} | all-to-all | bytes 524288 | tf_op jit(solution)/shard_map/all_to_all | solution.py:257
  26.6 3.5 %collective-permute-start = (bf16[128,128]{1,0:T(8,128)(2,1)S(1)}, bf16[128,128]{1,0:T(8,128)(2,1)S(1)}, u32[]{:S(2)}, u32[]{:S(2)}) collective-permute-start(bf16[128,128]{1,0:T(8,128)(2,1)S(1)} %shard_map.121), channel_id=1, source_target_pairs={{0,64},{64,128},{128,192},{1,65},{65,129},{129,193},{2,66},{66,130... | collective-permute-start | bytes 98312 | tf_op jit(solution)/shard_map/ppermute | solution.py:263
  30.1 2.0 %collective-permute-start.1 = (bf16[128,128]{1,0:T(8,128)(2,1)S(1)}, bf16[128,128]{1,0:T(8,128)(2,1)S(1)}, u32[]{:S(2)}, u32[]{:S(2)}) collective-permute-start(bf16[128,128]{1,0:T(8,128)(2,1)S(1)} %shard_map.121), channel_id=1, source_target_pairs={{0,128},{64,192},{1,129},{65,193},{2,130},{66,194},{3,131},{67,195... | collective-permute-start | bytes 98312 | tf_op jit(solution)/shard_map/ppermute | solution.py:263
  32.1 0.7 collective-permute-start.2
  32.8 0.0 collective-permute-done.t1_ref
  32.8 0.9 collective-permute-done.1.t2_ref
  33.7 0.0 collective-permute-done.2.t3_ref
  33.7 0.8 shard_map.122
  34.5 3.4 %all-to-all-start.1 = ((bf16[8,128,128]{2,1,0:T(8,128)(2,1)}), bf16[8,128,128]{2,1,0:T(8,128)(2,1)S(1)}, u32[]{:S(2)}, u32[]{:S(2)}) async-start(bf16[8,128,128]{2,1,0:T(8,128)(2,1)} %shard_map.122), calls=%async_computation.1 | async-start | bytes 524288 | tf_op jit(solution)/shard_map/all_to_all | solution.py:267
  37.9 0.0 copy-done.21
  37.9 0.0 copy-done.22
  37.9 0.7 pad_maximum_fusion.kv0_ref
  38.6 3.8 %collective-permute-start.3 = (bf16[2,512,128]{2,1,0:T(8,128)(2,1)}, bf16[2,512,128]{2,1,0:T(8,128)(2,1)}, u32[]{:S(2)}, u32[]{:S(2)}) collective-permute-start(bf16[2,512,128]{2,1,0:T(8,128)(2,1)} %pad_maximum_fusion.kv0_ref), channel_id=1, source_target_pairs={{0,8},{8,16},{16,24},{24,32},{32,40},{40,48},{48,56},{56,64},{64,7... | collective-permute-start | bytes 786440 | tf_op jit(solution)/shard_map/ppermute | solution.py:283
  42.5 0.0 copy-done.2
  42.5 0.0 copy-done.1
  42.5 0.0 copy-done.15
  42.5 0.0 copy-start.4
  42.5 1.2 copy-done.4
  43.7 1.2 copy-done.7
  44.9 4.3 %shard_map.120 = (bf16[8,512,128]{2,1,0:T(8,128)(2,1)S(1)}, f32[8,512,128]{2,1,0:T(8,128)}, f32[8,512,128]{2,1,0:T(8,128)}) custom-call(bf16[512,8,128]{2,1,0:T(8,128)(2,1)S(1)} %copy-done.1, bf16[512,8,128]{2,1,0:T(8,128)(2,1)S(1)} %copy-done.2, f32[8,128]{1,0:T(8,128)S(1)} %copy-done.15, bf16[8,512,128]{2,1,0:T(8,128)(2,1)S(1)} %copy-done.4, ...), custom_call_target="tpu_custom_call" | custom-call | flops 1073741824 | bytes 9441280 | tf_op jit(solution)/shard_map/pallas_call | solution.py:46
  49.3 0.4 all-to-all-done.1.pre_ref
  49.7 1.7 %copy-done = f32[8,512,128]{2,1,0:T(8,128)S(1)} copy-done((f32[8,512,128]{2,1,0:T(8,128)S(1)}, f32[8,512,128]{2,1,0:T(8,128)}, u32[]{:S(2)}) %copy-start) | copy-done | bytes 2097176
  51.4 2.7 %shard_map.123 = (f32[8,512,128]{2,1,0:T(8,128)S(1)}, f32[2,512]{1,0:T(2,128)S(1)}) custom-call(f32[8,512,128]{2,1,0:T(8,128)S(1)} %copy-done, bf16[8,512,128]{2,1,0:T(8,128)(2,1)S(1)} %get-tuple-element.24.qh_ref, f32[8,512,128]{2,1,0:T(8,128)} %get-tuple-element.25.gh_ref, bf16[8,128,128]{2,1,0:T(8,128)(2,1)S(1)} %all-to-all-done.1.pre_ref), custom_call_target="tpu_custom_call" | custom-call | flops 134217728 | bytes 7606272 | tf_op jit(solution)/shard_map/pallas_call | solution.py:46
  54.1 0.0 copy-done.12
  54.1 13.2 %all-gather.1.g_ref = f32[8,2,512]{2,1,0:T(2,128)S(1)} all-gather(f32[1,2,512]{2,1,0:T(2,128)S(1)} %bitcast.4), channel_id=2, replica_groups=mesh['y'=4,'z'=8,'x'=4,'core'=2] {'x','core'}, dimensions={0}, use_global_device_ids=true | all-gather | bytes 36864 | tf_op jit(solution)/shard_map/all_gather | solution.py:308
  67.3 3.1 %shard_map.124 = (bf16[8,512,128]{2,1,0:T(8,128)(2,1)S(1)}, bf16[8,128,128]{2,1,0:T(8,128)(2,1)S(1)}, f32[512,128]{1,0:T(8,128)S(1)}) custom-call(f32[8,2,512]{2,1,0:T(2,128)S(1)} %all-gather.1.g_ref, f32[8,512,128]{2,1,0:T(8,128)S(1)} %get-tuple-element.27.att_ref, f32[8,512,128]{2,1,0:T(8,128)} %get-tuple-element.25.gh_ref, ...), custom_call_target="tpu_custom_call" | custom-call | flops 134217728 | bytes 6848512 | tf_op jit(solution)/shard_map/pallas_call | solution.py:46
  70.4 0.0 copy-start.14
  70.4 0.7 copy-done.14
  71.1 1.0 copy-done.17
  72.1 0.7 copy-done.19
  72.8 6.7 %all-to-all-start.2 = ((bf16[8,128,128]{2,1,0:T(8,128)(2,1)}), bf16[8,128,128]{2,1,0:T(8,128)(2,1)S(1)}, u32[]{:S(2)}, u32[]{:S(2)}) async-start(bf16[8,128,128]{2,1,0:T(8,128)(2,1)} %copy-done.14), calls=%async_computation.2 | async-start | bytes 524288 | tf_op jit(solution)/shard_map/all_to_all | solution.py:257
  79.5 0.0 collective-permute-done.3.kv1_ref
  79.5 3.9 %collective-permute-start.4 = (bf16[2,512,128]{2,1,0:T(8,128)(2,1)}, bf16[2,512,128]{2,1,0:T(8,128)(2,1)}, u32[]{:S(2)}, u32[]{:S(2)}) collective-permute-start(bf16[2,512,128]{2,1,0:T(8,128)(2,1)} %collective-permute-done.3.kv1_ref), channel_id=1, source_target_pairs={{0,8},{8,16},{16,24},{24,32},{32,40},{40,48},{48,56},{56,64},{64,7... | collective-permute-start | bytes 786440 | tf_op jit(solution)/shard_map/ppermute | solution.py:283
  83.4 14.2 %collective-permute-done.4.kv2_ref = bf16[2,512,128]{2,1,0:T(8,128)(2,1)} collective-permute-done((bf16[2,512,128]{2,1,0:T(8,128)(2,1)}, bf16[2,512,128]{2,1,0:T(8,128)(2,1)}, u32[]{:S(2)}, u32[]{:S(2)}) %collective-permute-start.4) | collective-permute-done | bytes 262176 | tf_op jit(solution)/shard_map/ppermute | solution.py:283
  97.6 1.9 %collective-permute-start.5 = (bf16[2,512,128]{2,1,0:T(8,128)(2,1)}, bf16[2,512,128]{2,1,0:T(8,128)(2,1)}, u32[]{:S(2)}, u32[]{:S(2)}) collective-permute-start(bf16[2,512,128]{2,1,0:T(8,128)(2,1)} %collective-permute-done.4.kv2_ref), channel_id=1, source_target_pairs={{0,8},{8,16},{16,24},{24,32},{32,40},{40,48},{48,56},{56,64},{64,7... | collective-permute-start | bytes 786440 | tf_op jit(solution)/shard_map/ppermute | solution.py:283
  99.5 0.0 all-to-all-done.2.recv_ref
  99.5 2.2 %collective-permute-start.6 = (bf16[128,128]{1,0:T(8,128)(2,1)S(1)}, bf16[128,128]{1,0:T(8,128)(2,1)S(1)}, u32[]{:S(2)}, u32[]{:S(2)}) collective-permute-start(bf16[128,128]{1,0:T(8,128)(2,1)S(1)} %shard_map.126), channel_id=1, source_target_pairs={{64,0},{128,64},{192,128},{65,1},{129,65},{193,129},{66,2},{130,66... | collective-permute-start | bytes 98312 | tf_op jit(solution)/shard_map/ppermute | solution.py:263
  101.7 1.3 collective-permute-start.7
  103.0 0.7 collective-permute-start.8
  103.7 1.6 %collective-permute-done.6.t1_ref = bf16[128,128]{1,0:T(8,128)(2,1)S(1)} collective-permute-done((bf16[128,128]{1,0:T(8,128)(2,1)S(1)}, bf16[128,128]{1,0:T(8,128)(2,1)S(1)}, u32[]{:S(2)}, u32[]{:S(2)}) %collective-permute-start.6) | collective-permute-done | bytes 32800 | tf_op jit(solution)/shard_map/ppermute | solution.py:263
  105.3 3.7 %collective-permute-done.7.t2_ref = bf16[128,128]{1,0:T(8,128)(2,1)S(1)} collective-permute-done((bf16[128,128]{1,0:T(8,128)(2,1)S(1)}, bf16[128,128]{1,0:T(8,128)(2,1)S(1)}, u32[]{:S(2)}, u32[]{:S(2)}) %collective-permute-start.7) | collective-permute-done | bytes 32800 | tf_op jit(solution)/shard_map/ppermute | solution.py:263
  109.1 0.0 collective-permute-done.8.t3_ref
  109.1 0.1 shard_map.127
  109.1 0.7 copy-done.11
  109.8 6.2 %all-to-all-start.3 = ((bf16[8,128,128]{2,1,0:T(8,128)(2,1)}), bf16[8,128,128]{2,1,0:T(8,128)(2,1)}, u32[]{:S(2)}, u32[]{:S(2)}) async-start(bf16[8,128,128]{2,1,0:T(8,128)(2,1)} %copy-done.11), calls=%async_computation.3 | async-start | bytes 524288 | tf_op jit(solution)/shard_map/all_to_all | solution.py:267
  116.1 0.0 collective-permute-done.5.kv3_ref
  116.1 0.0 copy-start.16
  116.1 1.2 copy-done.16
  117.3 0.9 copy-done.20
  118.3 24.4 %shard_map.125 = (bf16[512,8,128]{2,1,0:T(8,128)(2,1)}, bf16[512,8,128]{2,1,0:T(8,128)(2,1)}) custom-call(s32[1]{0:T(128)} %bitcast.pos_ref, f32[8,512,128]{2,1,0:T(8,128)S(1)} %get-tuple-element.27.att_ref, f32[512,128]{1,0:T(8,128)S(1)} %copy-done.20, f32[8,128]{1,0:T(8,128)S(1)} %copy-done.15, bf16[512,8,128]{2,1,0:T(8,128)(2,1)S(1)} %copy-done.16, ...), custom_call_target="tpu_custom_call" | custom-call | flops 4294967296 | bytes 6557700 | tf_op jit(solution)/shard_map/pallas_call | solution.py:46
  142.7 0.0 all-to-all-done.3.suf_ref
  142.7 1.2 copy-done.5
  143.9 1.2 copy-done.8
  145.1 1.2 copy-done.18
  146.3 8.3 %shard_map.128 = (bf16[512,8,128]{2,1,0:T(8,128)(2,1)}, bf16[512,8,128]{2,1,0:T(8,128)(2,1)}, bf16[512,8,128]{2,1,0:T(8,128)(2,1)}) custom-call(bf16[8,512,128]{2,1,0:T(8,128)(2,1)S(1)} %get-tuple-element.24.qh_ref, bf16[8,512,128]{2,1,0:T(8,128)(2,1)S(1)} %copy-done.5, bf16[8,512,128]{2,1,0:T(8,128)(2,1)S(1)} %copy-done.8, ...), custom_call_target="tpu_custom_call" | custom-call | flops 3221225472 | bytes 7864320 | tf_op jit(solution)/shard_map/pallas_call | solution.py:46
  (19 shorter events, 0.1 us)
Async XLA Ops:
  0.6 41.8 %copy-start.2 = (bf16[512,8,128]{2,1,0:T(8,128)(2,1)S(1)}, bf16[512,8,128]{2,1,0:T(8,128)(2,1)}, u32[]{:S(2)}) copy-start(bf16[512,8,128]{2,1,0:T(8,128)(2,1)} %c_ref.1) | copy-start | bytes 3145732
  0.6 41.8 %copy-start.1 = (bf16[512,8,128]{2,1,0:T(8,128)(2,1)S(1)}, bf16[512,8,128]{2,1,0:T(8,128)(2,1)}, u32[]{:S(2)}) copy-start(bf16[512,8,128]{2,1,0:T(8,128)(2,1)} %q_ref.1) | copy-start | bytes 3145732
  0.7 1.4 copy-start.9
  2.0 1.2 copy-start.10
  3.3 34.6 %copy-start.21 = (bf16[512,1,128]{2,0,1:T(8,128)(2,1)S(1)}, bf16[512,1,128]{2,0,1:T(8,128)(2,1)}, u32[]{:S(2)}) copy-start(bf16[512,1,128]{2,0,1:T(8,128)(2,1)} %param.15) | copy-start | bytes 393220
  3.3 34.7 %copy-start.22 = (bf16[512,1,128]{2,0,1:T(8,128)(2,1)S(1)}, bf16[512,1,128]{2,0,1:T(8,128)(2,1)}, u32[]{:S(2)}) copy-start(bf16[512,1,128]{2,0,1:T(8,128)(2,1)} %param.14) | copy-start | bytes 393220
  3.3 39.2 %copy-start.15 = (f32[8,128]{1,0:T(8,128)S(1)}, f32[8,128]{1,0:T(8,128)}, u32[]{:S(2)}) copy-start(f32[8,128]{1,0:T(8,128)} %gain_ref.3) | copy-start | bytes 12292
  4.5 1.0 copy-start.3
  5.5 1.0 copy-start.6
  26.6 6.2 %collective-permute-start = (bf16[128,128]{1,0:T(8,128)(2,1)S(1)}, bf16[128,128]{1,0:T(8,128)(2,1)S(1)}, u32[]{:S(2)}, u32[]{:S(2)}) collective-permute-start(bf16[128,128]{1,0:T(8,128)(2,1)S(1)} %shard_map.121), channel_id=1, source_target_pairs={{0,64},{64,128},{128,192},{1,65},{65,129},{129,193},{2,66},{66,130... | collective-permute-start | bytes 98312 | tf_op jit(solution)/shard_map/ppermute | solution.py:263
  30.1 3.6 %collective-permute-start.1 = (bf16[128,128]{1,0:T(8,128)(2,1)S(1)}, bf16[128,128]{1,0:T(8,128)(2,1)S(1)}, u32[]{:S(2)}, u32[]{:S(2)}) collective-permute-start(bf16[128,128]{1,0:T(8,128)(2,1)S(1)} %shard_map.121), channel_id=1, source_target_pairs={{0,128},{64,192},{1,129},{65,193},{2,130},{66,194},{3,131},{67,195... | collective-permute-start | bytes 98312 | tf_op jit(solution)/shard_map/ppermute | solution.py:263
  32.1 1.6 %collective-permute-start.2 = (bf16[128,128]{1,0:T(8,128)(2,1)S(1)}, bf16[128,128]{1,0:T(8,128)(2,1)S(1)}, u32[]{:S(2)}, u32[]{:S(2)}) collective-permute-start(bf16[128,128]{1,0:T(8,128)(2,1)S(1)} %shard_map.121), channel_id=1, source_target_pairs={{0,192},{1,193},{2,194},{3,195},{4,196},{5,197},{6,198},{7,199},{8... | collective-permute-start | bytes 98312 | tf_op jit(solution)/shard_map/ppermute | solution.py:263
  34.5 15.2 %all-to-all-start.1 = ((bf16[8,128,128]{2,1,0:T(8,128)(2,1)}), bf16[8,128,128]{2,1,0:T(8,128)(2,1)S(1)}, u32[]{:S(2)}, u32[]{:S(2)}) async-start(bf16[8,128,128]{2,1,0:T(8,128)(2,1)} %shard_map.122), calls=%async_computation.1 | async-start | bytes 524288 | tf_op jit(solution)/shard_map/all_to_all | solution.py:267
  38.6 40.8 %collective-permute-start.3 = (bf16[2,512,128]{2,1,0:T(8,128)(2,1)}, bf16[2,512,128]{2,1,0:T(8,128)(2,1)}, u32[]{:S(2)}, u32[]{:S(2)}) collective-permute-start(bf16[2,512,128]{2,1,0:T(8,128)(2,1)} %pad_maximum_fusion.kv0_ref), channel_id=1, source_target_pairs={{0,8},{8,16},{16,24},{24,32},{32,40},{40,48},{48,56},{56,64},{64,7... | collective-permute-start | bytes 786440 | tf_op jit(solution)/shard_map/ppermute | solution.py:283
  42.5 1.2 copy-start.4
  43.7 1.2 copy-start.7
  49.7 4.4 %copy-start.12 = (bf16[8,128,128]{2,1,0:T(8,128)(2,1)}, bf16[8,128,128]{2,1,0:T(8,128)(2,1)S(1)}, u32[]{:S(2)}) copy-start(bf16[8,128,128]{2,1,0:T(8,128)(2,1)S(1)} %all-to-all-done.1.pre_ref) | copy-start | bytes 786436
  49.7 1.7 %copy-start = (f32[8,512,128]{2,1,0:T(8,128)S(1)}, f32[8,512,128]{2,1,0:T(8,128)}, u32[]{:S(2)}) copy-start(f32[8,512,128]{2,1,0:T(8,128)} %get-tuple-element.23.loc_ref) | copy-start | bytes 6291460
  70.4 0.7 copy-start.14
  71.1 1.0 copy-start.17
  72.1 0.7 copy-start.19
  72.8 26.7 %all-to-all-start.2 = ((bf16[8,128,128]{2,1,0:T(8,128)(2,1)}), bf16[8,128,128]{2,1,0:T(8,128)(2,1)S(1)}, u32[]{:S(2)}, u32[]{:S(2)}) async-start(bf16[8,128,128]{2,1,0:T(8,128)(2,1)} %copy-done.14), calls=%async_computation.2 | async-start | bytes 524288 | tf_op jit(solution)/shard_map/all_to_all | solution.py:257
  79.5 18.1 %collective-permute-start.4 = (bf16[2,512,128]{2,1,0:T(8,128)(2,1)}, bf16[2,512,128]{2,1,0:T(8,128)(2,1)}, u32[]{:S(2)}, u32[]{:S(2)}) collective-permute-start(bf16[2,512,128]{2,1,0:T(8,128)(2,1)} %collective-permute-done.3.kv1_ref), channel_id=1, source_target_pairs={{0,8},{8,16},{16,24},{24,32},{32,40},{40,48},{48,56},{56,64},{64,7... | collective-permute-start | bytes 786440 | tf_op jit(solution)/shard_map/ppermute | solution.py:283
  97.6 18.5 %collective-permute-start.5 = (bf16[2,512,128]{2,1,0:T(8,128)(2,1)}, bf16[2,512,128]{2,1,0:T(8,128)(2,1)}, u32[]{:S(2)}, u32[]{:S(2)}) collective-permute-start(bf16[2,512,128]{2,1,0:T(8,128)(2,1)} %collective-permute-done.4.kv2_ref), channel_id=1, source_target_pairs={{0,8},{8,16},{16,24},{24,32},{32,40},{40,48},{48,56},{56,64},{64,7... | collective-permute-start | bytes 786440 | tf_op jit(solution)/shard_map/ppermute | solution.py:283
  99.5 5.8 %collective-permute-start.6 = (bf16[128,128]{1,0:T(8,128)(2,1)S(1)}, bf16[128,128]{1,0:T(8,128)(2,1)S(1)}, u32[]{:S(2)}, u32[]{:S(2)}) collective-permute-start(bf16[128,128]{1,0:T(8,128)(2,1)S(1)} %shard_map.126), channel_id=1, source_target_pairs={{64,0},{128,64},{192,128},{65,1},{129,65},{193,129},{66,2},{130,66... | collective-permute-start | bytes 98312 | tf_op jit(solution)/shard_map/ppermute | solution.py:263
  101.7 7.3 %collective-permute-start.7 = (bf16[128,128]{1,0:T(8,128)(2,1)S(1)}, bf16[128,128]{1,0:T(8,128)(2,1)S(1)}, u32[]{:S(2)}, u32[]{:S(2)}) collective-permute-start(bf16[128,128]{1,0:T(8,128)(2,1)S(1)} %shard_map.126), channel_id=1, source_target_pairs={{128,0},{192,64},{129,1},{193,65},{130,2},{194,66},{131,3},{195,67... | collective-permute-start | bytes 98312 | tf_op jit(solution)/shard_map/ppermute | solution.py:263
  103.0 6.0 %collective-permute-start.8 = (bf16[128,128]{1,0:T(8,128)(2,1)S(1)}, bf16[128,128]{1,0:T(8,128)(2,1)S(1)}, u32[]{:S(2)}, u32[]{:S(2)}) collective-permute-start(bf16[128,128]{1,0:T(8,128)(2,1)S(1)} %shard_map.126), channel_id=1, source_target_pairs={{192,0},{193,1},{194,2},{195,3},{196,4},{197,5},{198,6},{199,7},{2... | collective-permute-start | bytes 98312 | tf_op jit(solution)/shard_map/ppermute | solution.py:263
  109.1 0.7 copy-start.11
  109.8 32.8 %all-to-all-start.3 = ((bf16[8,128,128]{2,1,0:T(8,128)(2,1)}), bf16[8,128,128]{2,1,0:T(8,128)(2,1)}, u32[]{:S(2)}, u32[]{:S(2)}) async-start(bf16[8,128,128]{2,1,0:T(8,128)(2,1)} %copy-done.11), calls=%async_computation.3 | async-start | bytes 524288 | tf_op jit(solution)/shard_map/all_to_all | solution.py:267
  116.1 1.2 copy-start.16
  117.3 0.9 copy-start.20
  118.3 24.4 %copy-start.13 = (bf16[8,128,128]{2,1,0:T(8,128)(2,1)S(1)}, bf16[8,128,128]{2,1,0:T(8,128)(2,1)}, u32[]{:S(2)}) copy-start(bf16[8,128,128]{2,1,0:T(8,128)(2,1)} %copy-done.12) | copy-start | bytes 786436
  142.7 1.2 copy-start.5
  143.9 1.2 copy-start.8
  145.1 1.2 copy-start.18
